TPU v7x, 32 devices: a whole 2x2x4 slice. The times are simulated.
32 devices in a mesh: dp: 8 (over z, y), mp: 4 (over x, core).
Axes of the slice: x: 2, y: 2, z: 4, core: 2. Of those that a mesh axis runs over, the one named last changes fastest.
Arguments:
- item_table: bfloat16 [16384, 256], P('dp'), may hold values from -6 to 6
- history_owner: int32 [2048, 1], P(('dp', 'mp')), may hold values from 0 to 7; in each aligned block of 64 rows (0 to 63, 64 to 127, ...) at most 16 rows name the same one
- history_row: int32 [2048], P(('dp', 'mp')), may hold values from 0 to 2047
- w_in: bfloat16 [256, 512], replicated, may hold values from -0.375 to 0.375
- conv_a: bfloat16 [4, 3, 512, 512], P(None, None, None, 'mp'), may hold values from -0.15625 to 0.15625
- conv_b: bfloat16 [4, 3, 512, 512], P(None, None, 'mp'), may hold values from -0.15625 to 0.15625
- gains: float32 [4, 512], replicated, may hold values from 0.5 to 1.5
- w_out: bfloat16 [512, 256], replicated, may hold values from -0.25 to 0.25
- cand_row: int32 [8, 8, 8], P('dp'), may hold values from 0 to 2047
- cand_count: int32 [8, 8], P('dp'), may hold values from 1 to 8, 32 in all within a row
- pos_owner: int32 [8], P('dp'), may hold values from 0 to 7
Outputs:
- scores: float32 [8, 8, 8], P('dp')
- user_loss: float32 [8], P('dp')
Inputs may be any that keep to these rules, and one draw needn't show every extreme that they name: `history_owner`: within each aligned block of 64 events no owner appears more than 16 times, and some owner appears exactly 16 times. `cand_count`: each user's counts sum to 32; the largest of them is 8.
All inputs are finite; a program needn't handle non-finite values.
Results may differ from a plain program's by a relative error of at most 0.025.
Values may be sent and summed in bfloat16 or wider, within the bound.
A program may use at most 64 MiB of HBM per device.

v0:
```python
import jax
import jax.numpy as jnp
from jax import lax
from jax.sharding import PartitionSpec as P

C = 512
BLOCKS = 4
LEN = 256


def shift_rows(values, offset):
    padded = jnp.pad(values, ((0, 0), (offset, 0), (0, 0)))
    return padded[:, : values.shape[1], :]


def causal_taps(values, dilation):
    return jnp.concatenate(
        [values, shift_rows(values, dilation), shift_rows(values, 2 * dilation)], axis=-1
    )


def lookup(item_table, owner_ids, row_ids, fetch_len, capacity, dp_count):
    groups = owner_ids.shape[0] // fetch_len
    owner_grid = owner_ids.reshape(groups, fetch_len)
    onehot = (
        owner_grid[:, :, None] == jnp.arange(dp_count, dtype=jnp.int32)[None, None, :]
    ).astype(jnp.int32)
    before = jnp.cumsum(onehot, axis=1) - onehot
    slot_within = jnp.sum(before * onehot, axis=2)
    slot_ids = (slot_within + jnp.arange(groups, dtype=jnp.int32)[:, None] * capacity).reshape(-1)
    flat_owner = owner_grid.reshape(-1)
    requests = (
        jnp.zeros((groups * capacity, dp_count), jnp.int32).at[slot_ids, flat_owner].set(row_ids)
    )
    picked = item_table[lax.all_to_all(requests, "dp", split_axis=1, concat_axis=1, tiled=True)]
    arrived = lax.all_to_all(picked, "dp", split_axis=1, concat_axis=1, tiled=True)
    return arrived[slot_ids, flat_owner]


def per_device(
    item_table,
    history_owner,
    history_row,
    w_in,
    conv_a,
    conv_b,
    gains,
    w_out,
    cand_row,
    cand_count,
    pos_owner,
):
    dp_count = lax.axis_size("dp")
    mp_count = lax.axis_size("mp")
    fetch_len = history_row.shape[0]
    capacity = max(4, 2 * fetch_len // dp_count)
    owner_ids = history_owner[:, 0]
    embedded = lookup(item_table, owner_ids, history_row, fetch_len, capacity, dp_count)
    embedded = lax.all_gather(embedded, "mp", axis=0, tiled=True)
    user_count = cand_row.shape[0]
    hidden = jnp.dot(embedded, w_in, preferred_element_type=jnp.float32).astype(jnp.bfloat16)
    quarter = C // mp_count
    mp_index = lax.axis_index("mp")
    for block_idx in range(BLOCKS):
        dilation = 1 if block_idx % 2 == 0 else 4
        taps_a = causal_taps(hidden.reshape(user_count, LEN, C), dilation).reshape(-1, 3 * C)
        rectified = jax.nn.relu(
            jnp.dot(
                taps_a,
                conv_a[block_idx].reshape(3 * C, quarter),
                preferred_element_type=jnp.float32,
            )
        ).astype(jnp.bfloat16)
        taps_b = causal_taps(rectified.reshape(user_count, LEN, quarter), 2 * dilation).reshape(
            -1, 3 * quarter
        )
        partial_value = jnp.dot(
            taps_b, conv_b[block_idx].reshape(3 * quarter, C), preferred_element_type=jnp.float32
        )
        gain_row = gains[block_idx]
        share = lax.psum_scatter(
            partial_value.astype(jnp.bfloat16), "mp", scatter_dimension=1, tiled=True
        ).astype(jnp.float32)
        base = lax.dynamic_slice_in_dim(hidden, mp_index * quarter, quarter, 1).astype(jnp.float32)
        summed = base + share
        row_sum, row_sq = lax.psum(
            (jnp.sum(summed, axis=1), jnp.sum(summed * summed, axis=1)), "mp"
        )
        row_mean = (row_sum / C)[:, None]
        row_var = (row_sq / C)[:, None] - row_mean * row_mean
        gain_part = lax.dynamic_slice_in_dim(gain_row, mp_index * quarter, quarter, 0)
        normed = ((summed - row_mean) * lax.rsqrt(row_var + 1e-05) * gain_part).astype(jnp.bfloat16)
        hidden = lax.all_gather(normed, "mp", axis=1, tiled=True)
    last_rows = hidden.reshape(user_count, LEN, C)[:, LEN - 1, :]
    user_vec = jnp.dot(last_rows, w_out, preferred_element_type=jnp.float32).astype(jnp.bfloat16)
    cand_rows = lax.all_to_all(
        item_table[lax.all_to_all(cand_row, "dp", split_axis=1, concat_axis=1, tiled=True)],
        "dp",
        split_axis=1,
        concat_axis=1,
        tiled=True,
    )
    raw_scores = 0.25 * jnp.einsum(
        "ue,unce->unc", user_vec, cand_rows, preferred_element_type=jnp.float32
    )
    valid_slot = (
        jnp.arange(raw_scores.shape[2], dtype=jnp.int32)[None, None, :] < cand_count[:, :, None]
    )
    scores = jnp.where(valid_slot, raw_scores, 0.0)
    exp_total = jnp.sum(jnp.where(valid_slot, jnp.exp(raw_scores), 0.0), axis=(1, 2))
    positive = jnp.take_along_axis(raw_scores[:, :, 0], pos_owner[:, None], axis=1)[:, 0]
    user_loss = jnp.log(exp_total) - positive
    return (scores, user_loss)


def solution(mesh):
    return jax.shard_map(
        per_device,
        mesh=mesh,
        in_specs=(
            P("dp", None),
            P(("dp", "mp"), None),
            P(("dp", "mp")),
            P(),
            P(None, None, None, "mp"),
            P(None, None, "mp", None),
            P(),
            P(),
            P("dp", None, None),
            P("dp", None),
            P("dp"),
        ),
        out_specs=(P("dp", None, None), P("dp")),
        check_vma=False,
    )
```

profile of v0, /device:TPU:0, one launch (start us, length us, event | category | flops | bytes accessed | tf_op | source)
XLA Modules:
  0.0 205.7 jit_solution(13466684833797918691)
XLA Ops:
  7.2 0.8 fusion.46
  8.1 0.8 select_reduce_fusion
  8.9 0.7 fusion.54
  9.6 0.6 broadcast.145
  10.2 10.2 %scatter_fusion = s32[16,8]{0,1:T(8,128)} fusion(s32[16,8]{0,1:T(8,128)} %broadcast.145, s32[64]{0:T(128)S(1)} %get-tuple-element.29, s32[64]{0:T(128)} %param.13), kind=kCustom, calls=%fused_computation.3 | custom fusion | bytes 1280 | tf_op jit(solution)/shard_map/scatter | solution.py:33
  20.4 7.3 %all-to-all-start = ((s32[16,8,1]{0,2,1:T(1,128)}), s32[16,8,1]{0,2,1:T(1,128)S(1)}, u32[]{:S(2)}, u32[]{:S(2)}) async-start(s32[16,8,1]{0,2,1:T(1,128)} %bitcast.5), calls=%async_computation | async-start | bytes 8192 | tf_op jit(solution)/shard_map/all_to_all | solution.py:35
  27.7 2.5 %fusion.64 = (bf16[1,3,512,128]{3,2,1,0:T(8,128)(2,1)}, bf16[1,3,512,128]{3,2,1,0:T(8,128)(2,1)}, bf16[1,3,512,128]{3,2,1,0:T(8,128)(2,1)S(1)}, bf16[1,3,512,128]{3,2,1,0:T(8,128)(2,1)}) fusion(bf16[4,3,512,128]{3,2,1,0:T(8,128)(2,1)} %param.15), kind=kLoop, calls=%fused_computation.141 | loop fusion | bytes 3145728 | tf_op jit(solution)/shard_map/slice | solution.py:70
  30.2 3.9 %all-to-all-done = s32[16,8,1]{0,2,1:T(1,128)S(1)} async-done(((s32[16,8,1]{0,2,1:T(1,128)}), s32[16,8,1]{0,2,1:T(1,128)S(1)}, u32[]{:S(2)}, u32[]{:S(2)}) %all-to-all-start) | async-done | bytes 544 | tf_op jit(solution)/shard_map/all_to_all | solution.py:35
  34.3 0.8 gather_fusion
  35.1 0.6 copy.23
  35.8 3.3 %all-to-all-start.1 = ((bf16[16,8,256]{2,0,1:T(8,128)(2,1)}), bf16[16,8,256]{2,0,1:T(8,128)(2,1)S(1)}, u32[]{:S(2)}, u32[]{:S(2)}) async-start(bf16[16,8,256]{2,0,1:T(8,128)(2,1)} %copy.23), calls=%async_computation.1 | async-start | bytes 131072 | tf_op jit(solution)/shard_map/all_to_all | solution.py:36
  39.2 1.0 fusion.65
  40.2 5.7 %all-to-all-done.1 = bf16[16,8,256]{2,0,1:T(8,128)(2,1)S(1)} async-done(((bf16[16,8,256]{2,0,1:T(8,128)(2,1)}), bf16[16,8,256]{2,0,1:T(8,128)(2,1)S(1)}, u32[]{:S(2)}, u32[]{:S(2)}) %all-to-all-start.1) | async-done | bytes 65568 | tf_op jit(solution)/shard_map/all_to_all | solution.py:36
  46.0 0.8 gather_fusion.1
  46.8 5.4 %all_gather.15 = bf16[256,256]{1,0:T(8,128)(2,1)S(1)} all-gather(bf16[64,256]{1,0:T(8,128)(2,1)S(1)} %gather_fusion.1), channel_id=1, replica_groups=mesh['dp'=8,'mp'=4] {'mp'}, dimensions={0}, use_global_device_ids=true | all-gather | bytes 163840 | tf_op jit(solution)/shard_map/all_gather | solution.py:59
  52.2 1.2 convolution_convert_fusion.4
  53.5 0.4 fusion.7
  53.9 0.6 copy-done.7
  54.8 0.8 copy.28
  55.8 17.6 %reduce-scatter.13.cloned.1.call-done = bf16[128,256]{1,0:T(8,128)(2,1)} async-done(((bf16[512,256]{1,0:T(8,128)(2,1)}), bf16[128,256]{1,0:T(8,128)(2,1)}) %reduce-scatter.13.cloned.1.call-update) | async-done | bytes 65552
  73.3 0.9 copy.29
  74.5 5.8 %all-reduce.19 = (f32[256]{0:T(256)S(1)}, f32[256]{0:T(256)S(1)}) all-reduce(f32[256]{0:T(256)S(1)} %get-tuple-element.20, f32[256]{0:T(256)S(1)} %get-tuple-element.19), channel_id=1, replica_groups=mesh['dp'=8,'mp'=4] {'mp'}, use_global_device_ids=true, to_apply=%region_7.8 | all-reduce | flops 512 | bytes 4096 | tf_op jit(solution)/shard_map/psum | solution.py:86
  80.4 5.8 %all_gather.16 = bf16[256,512]{1,0:T(8,128)(2,1)S(1)} all-gather(bf16[256,128]{1,0:T(8,128)(2,1)S(1)} %multiply_convert_fusion.3), channel_id=1, replica_groups=mesh['dp'=8,'mp'=4] {'mp'}, dimensions={1}, use_global_device_ids=true | all-gather | bytes 327680 | tf_op jit(solution)/shard_map/all_gather | solution.py:93
  86.3 0.4 fusion.6
  86.7 0.6 copy-done.5
  87.6 0.9 copy.30
  88.5 21.2 %reduce-scatter.15.cloned.1.call-done = bf16[128,256]{1,0:T(8,128)(2,1)} async-done(((bf16[512,256]{1,0:T(8,128)(2,1)}), bf16[128,256]{1,0:T(8,128)(2,1)}) %reduce-scatter.15.cloned.1.call-update) | async-done | bytes 65552
  109.7 0.9 copy.31
  110.8 5.8 %all-reduce.18 = (f32[256]{0:T(256)S(1)}, f32[256]{0:T(256)S(1)}) all-reduce(f32[256]{0:T(256)S(1)} %get-tuple-element.18, f32[256]{0:T(256)S(1)} %get-tuple-element.17), channel_id=1, replica_groups=mesh['dp'=8,'mp'=4] {'mp'}, use_global_device_ids=true, to_apply=%region_12.13 | all-reduce | flops 512 | bytes 4096 | tf_op jit(solution)/shard_map/psum | solution.py:86
  116.7 5.9 %all_gather.17 = bf16[256,512]{1,0:T(8,128)(2,1)S(1)} all-gather(bf16[256,128]{1,0:T(8,128)(2,1)S(1)} %multiply_convert_fusion.2), channel_id=1, replica_groups=mesh['dp'=8,'mp'=4] {'mp'}, dimensions={1}, use_global_device_ids=true | all-gather | bytes 327680 | tf_op jit(solution)/shard_map/all_gather | solution.py:93
  122.8 0.4 fusion.5
  123.2 0.6 copy-done.3
  124.0 0.8 copy.32
  125.0 21.1 %reduce-scatter.17.cloned.1.call-done = bf16[128,256]{1,0:T(8,128)(2,1)} async-done(((bf16[512,256]{1,0:T(8,128)(2,1)}), bf16[128,256]{1,0:T(8,128)(2,1)}) %reduce-scatter.17.cloned.1.call-update) | async-done | bytes 65552
  146.1 0.9 copy.33
  147.2 5.8 %all-reduce.17 = (f32[256]{0:T(256)S(1)}, f32[256]{0:T(256)S(1)}) all-reduce(f32[256]{0:T(256)S(1)} %get-tuple-element.16, f32[256]{0:T(256)S(1)} %get-tuple-element.15), channel_id=1, replica_groups=mesh['dp'=8,'mp'=4] {'mp'}, use_global_device_ids=true, to_apply=%region_17.18 | all-reduce | flops 512 | bytes 4096 | tf_op jit(solution)/shard_map/psum | solution.py:86
  153.1 5.9 %all_gather.18 = bf16[256,512]{1,0:T(8,128)(2,1)S(1)} all-gather(bf16[256,128]{1,0:T(8,128)(2,1)S(1)} %multiply_convert_fusion.1), channel_id=1, replica_groups=mesh['dp'=8,'mp'=4] {'mp'}, dimensions={1}, use_global_device_ids=true | all-gather | bytes 327680 | tf_op jit(solution)/shard_map/all_gather | solution.py:93
  159.8 0.8 copy.34
  160.7 5.6 %all-to-all-start.2 = ((s32[1,8,8]{2,0,1:T(1,128)}), s32[1,8,8]{2,0,1:T(1,128)S(1)}, u32[]{:S(2)}, u32[]{:S(2)}) async-start(s32[1,8,8]{2,0,1:T(1,128)} %bitcast.38), calls=%async_computation.2 | async-start | bytes 8192 | tf_op jit(solution)/shard_map/all_to_all | solution.py:97
  167.0 5.7 %all-to-all-done.2 = s32[1,8,8]{2,0,1:T(1,128)S(1)} async-done(((s32[1,8,8]{2,0,1:T(1,128)}), s32[1,8,8]{2,0,1:T(1,128)S(1)}, u32[]{:S(2)}, u32[]{:S(2)}) %all-to-all-start.2) | async-done | bytes 288 | tf_op jit(solution)/shard_map/all_to_all | solution.py:97
  172.8 1.3 gather_fusion.2
  174.1 3.3 %all-to-all-start.3 = ((bf16[1,8,8,256]{3,2,0,1:T(8,128)(2,1)}), bf16[1,8,8,256]{3,2,0,1:T(8,128)(2,1)S(1)}, u32[]{:S(2)}, u32[]{:S(2)}) async-start(bf16[1,8,8,256]{3,2,0,1:T(8,128)(2,1)} %bitcast.40), calls=%async_computation.3 | async-start | bytes 65536 | tf_op jit(solution)/shard_map/all_to_all | solution.py:96
  177.4 4.1 %reduce-scatter.19.cloned.1.call-done = bf16[128,256]{1,0:T(8,128)(2,1)} async-done(((bf16[512,256]{1,0:T(8,128)(2,1)}), bf16[128,256]{1,0:T(8,128)(2,1)}) %reduce-scatter.19.cloned.1.call-update) | async-done | bytes 65552
  181.5 0.9 copy.35
  182.6 5.8 %all-reduce.16 = (f32[256]{0:T(256)S(1)}, f32[256]{0:T(256)S(1)}) all-reduce(f32[256]{0:T(256)S(1)} %get-tuple-element.14, f32[256]{0:T(256)S(1)} %get-tuple-element.13), channel_id=1, replica_groups=mesh['dp'=8,'mp'=4] {'mp'}, use_global_device_ids=true, to_apply=%region_22.23 | all-reduce | flops 512 | bytes 4096 | tf_op jit(solution)/shard_map/psum | solution.py:86
  188.5 5.9 %all_gather.19 = bf16[256,512]{1,0:T(8,128)(2,1)S(1)} all-gather(bf16[256,128]{1,0:T(8,128)(2,1)S(1)} %multiply_convert_fusion), channel_id=1, replica_groups=mesh['dp'=8,'mp'=4] {'mp'}, dimensions={1}, use_global_device_ids=true | all-gather | bytes 327680 | tf_op jit(solution)/shard_map/all_gather | solution.py:93
  194.8 1.3 select_reduce_fusion.1
  196.8 0.6 constant_dynamic-slice_fusion
  (71 shorter events, 4.2 us)
Async XLA Ops:
  7.2 27.1 %copy-start = (bf16[2048,256]{1,0:T(8,128)(2,1)S(1)}, bf16[2048,256]{1,0:T(8,128)(2,1)}, u32[]{:S(2)}) copy-start(bf16[2048,256]{1,0:T(8,128)(2,1)} %param.11) | copy-start | bytes 3145732
  20.4 13.7 %all-to-all-start = ((s32[16,8,1]{0,2,1:T(1,128)}), s32[16,8,1]{0,2,1:T(1,128)S(1)}, u32[]{:S(2)}, u32[]{:S(2)}) async-start(s32[16,8,1]{0,2,1:T(1,128)} %bitcast.5), calls=%async_computation | async-start | bytes 8192 | tf_op jit(solution)/shard_map/all_to_all | solution.py:35
  27.7 11.5 %copy-start.1 = (bf16[4,3,128,512]{3,2,1,0:T(8,128)(2,1)S(1)}, bf16[4,3,128,512]{3,2,1,0:T(8,128)(2,1)}, u32[]{:S(2)}) copy-start(bf16[4,3,128,512]{3,2,1,0:T(8,128)(2,1)} %param.16) | copy-start | bytes 4718596
  35.8 10.2 %all-to-all-start.1 = ((bf16[16,8,256]{2,0,1:T(8,128)(2,1)}), bf16[16,8,256]{2,0,1:T(8,128)(2,1)S(1)}, u32[]{:S(2)}, u32[]{:S(2)}) async-start(bf16[16,8,256]{2,0,1:T(8,128)(2,1)} %copy.23), calls=%async_computation.1 | async-start | bytes 131072 | tf_op jit(solution)/shard_map/all_to_all | solution.py:36
  39.1 34.2 %reduce-scatter.13.cloned.1.call-start = ((), (), s32[]{:S(2)}) async-start(), calls=%async_computation.8 | async-start | bytes 327680
  40.2 13.3 %copy-start.6 = (bf16[1,3,512,128]{3,2,1,0:T(8,128)(2,1)S(1)}, bf16[1,3,512,128]{3,2,1,0:T(8,128)(2,1)}, u32[]{:S(2)}) copy-start(bf16[1,3,512,128]{3,2,1,0:T(8,128)(2,1)} %get-tuple-element.31) | copy-start | bytes 1179652
  53.5 1.0 copy-start.7
  53.9 1.8 copy-start.9
  54.5 31.8 %copy-start.4 = (bf16[1,3,512,128]{3,2,1,0:T(8,128)(2,1)S(1)}, bf16[1,3,512,128]{3,2,1,0:T(8,128)(2,1)}, u32[]{:S(2)}) copy-start(bf16[1,3,512,128]{3,2,1,0:T(8,128)(2,1)} %get-tuple-element.32) | copy-start | bytes 1179652
  55.7 54.0 %reduce-scatter.15.cloned.1.call-start = ((), (), s32[]{:S(2)}) async-start(), calls=%async_computation.9 | async-start | bytes 327680
  86.3 1.0 copy-start.5
  87.3 35.5 %copy-start.2 = (bf16[1,3,512,128]{3,2,1,0:T(8,128)(2,1)S(1)}, bf16[1,3,512,128]{3,2,1,0:T(8,128)(2,1)}, u32[]{:S(2)}) copy-start(bf16[1,3,512,128]{3,2,1,0:T(8,128)(2,1)} %get-tuple-element.34) | copy-start | bytes 1179652
  88.4 57.6 %reduce-scatter.17.cloned.1.call-start = ((), (), s32[]{:S(2)}) async-start(), calls=%async_computation.10 | async-start | bytes 327680
  122.7 1.0 copy-start.3
  124.9 56.6 %reduce-scatter.19.cloned.1.call-start = ((), (), s32[]{:S(2)}) async-start(), calls=%async_computation.11 | async-start | bytes 327680
  159.4 35.0 %copy-start.8 = (bf16[512,256]{1,0:T(8,128)(2,1)S(1)}, bf16[512,256]{1,0:T(8,128)(2,1)}, u32[]{:S(2)}) copy-start(bf16[512,256]{1,0:T(8,128)(2,1)} %param.18) | copy-start | bytes 786436
  159.5 35.3 %copy-start.10 = (s32[1,8]{1,0:T(1,128)S(1)}, s32[1,8]{1,0:T(1,128)}, u32[]{:S(2)}) copy-start(s32[1,8]{1,0:T(1,128)} %param.20) | copy-start | bytes 100
  160.7 12.0 %all-to-all-start.2 = ((s32[1,8,8]{2,0,1:T(1,128)}), s32[1,8,8]{2,0,1:T(1,128)S(1)}, u32[]{:S(2)}, u32[]{:S(2)}) async-start(s32[1,8,8]{2,0,1:T(1,128)} %bitcast.38), calls=%async_computation.2 | async-start | bytes 8192 | tf_op jit(solution)/shard_map/all_to_all | solution.py:97
  174.1 20.5 %all-to-all-start.3 = ((bf16[1,8,8,256]{3,2,0,1:T(8,128)(2,1)}), bf16[1,8,8,256]{3,2,0,1:T(8,128)(2,1)S(1)}, u32[]{:S(2)}, u32[]{:S(2)}) async-start(bf16[1,8,8,256]{3,2,0,1:T(8,128)(2,1)} %bitcast.40), calls=%async_computation.3 | async-start | bytes 65536 | tf_op jit(solution)/shard_map/all_to_all | solution.py:96
Sparse Core Ops, SparseCore 0:
  55.8 17.5 reduce-scatter.12
  88.6 21.0 reduce-scatter.14
  125.0 21.0 reduce-scatter.16
  160.8 20.6 reduce-scatter.18
where the time goes:
time: 207 us; the launch traced here: 206 us
  waiting for transfers between devices  79.3 us (38%)
  blocking collectives  52 us (25%)
  local copies, waits for them, and re-layouts  28.2 us (14%)
  starting transfers between devices  19.7 us (10%)
  between operations  17.3 us (8%)
  other arithmetic  4.98 us (2%)
  matrix products  4.08 us (2%)
    unnamed x8, waiting for transfers between devices  64 us
    all_gather x4, blocking collectives, per_device(): hidden = lax.all_gather(normed, 'mp', axis=1, tiled=True)  23.5 us
    psum x4, blocking collectives, per_device(): lax.psum((jnp.sum(summed, axis=1), jnp.sum(summed * summed, axis=1)), 'mp')  23 us
    scatter x1, local copies, waits for them, and re-layouts, lookup(): jnp.zeros((groups * capacity, dp_count), jnp.int32).at[slot_ids, flat_owner]  10.2 us
    unnamed x30, local copies, waits for them, and re-layouts  8.92 us
    all_to_all x1, starting transfers between devices, lookup(): lax.all_to_all(requests, 'dp', split_axis=1, concat_axis=1, tiled=True)  7.28 us
    all_to_all x1, waiting for transfers between devices, lookup(): lax.all_to_all(picked, 'dp', split_axis=1, concat_axis=1, tiled=True)  5.73 us
    all_to_all x1, waiting for transfers between devices, per_device(): lax.all_to_all(cand_row, 'dp', split_axis=1, concat_axis=1, tiled=True)  5.71 us
  transfers between devices with their start and end apart: 8, of which 7 were waited for; matrix products, arithmetic and copies ran while one was open for 3% of the time, Pallas kernels for 0%

commit v1 on v0

v1 whole, which is shorter than its diff:
```python
import functools

import jax
import jax.numpy as jnp
from jax import lax
from jax.experimental import pallas as pl
from jax.experimental.pallas import tpu as pltpu
from jax.sharding import PartitionSpec as P

MESH = pl.DeviceIdType.MESH
DILATIONS = (1, 4, 1, 4)
F32 = jnp.float32
BF16 = jnp.bfloat16


def round_up(value, step):
    return -(-value // step) * step


def iota(shape, axis):
    return lax.broadcasted_iota(jnp.int32, shape, axis)


def rows_after(block):
    return round_up(1 + 6 * sum(DILATIONS[block + 1 :]), 16)


def kernel(
    dp, mp, capacity, cand_at, slots,
    owner_ref, row_ref, cand_ref, count_ref, pos_ref, gains_ref,
    table_hbm, w_in_hbm, conv_a_hbm, conv_b_hbm, w_out_hbm,
    scores_ref, loss_ref,
    table, w_in, conv_a, conv_b, w_out,
    message, requests, picked, arrived, parts0, parts1, parts2, parts3,
    load_sem, ask_send, ask_recv, row_send, row_recv, part_send, part_recv,
):
    user = lax.axis_index("dp")
    part = lax.axis_index("mp")
    fetch = owner_ref.shape[0]
    width = message.shape[2]
    cpo = cand_ref.shape[2]
    last = mp - 1

    loads = [
        pltpu.make_async_copy(source, target, load_sem.at[i])
        for i, (source, target) in enumerate(
            [(table_hbm, table), (w_in_hbm, w_in), (conv_a_hbm, conv_a),
             (conv_b_hbm, conv_b), (w_out_hbm, w_out)]
        )
    ]
    for load in loads:
        load.start()

    barrier = pltpu.get_barrier_semaphore()

    def greet(u, p):
        pl.semaphore_signal(barrier, inc=1, device_id=(u, p), device_id_type=MESH)

    def other_user(step):
        return lax.rem(user + step, dp)

    def other_part(step):
        return lax.rem(part + step, mp)

    def greet_same_part(step, _):
        greet(other_user(step), part)
        return 0

    def greet_askers(step, _):
        greet(other_user(step), last)
        return 0

    lax.fori_loop(1, dp, greet_same_part, 0)
    for step in range(1, mp):
        greet(user, other_part(step))

    @pl.when(part != last)
    def _():
        lax.fori_loop(1, dp, greet_askers, 0)

    @pl.when(part == last)
    def _():
        owner_col = owner_ref[...]
        square = (fetch, fetch)
        t_col, t_row = iota(square, 0), iota(square, 1)
        owner_row = jnp.sum(
            jnp.where(t_col == t_row, owner_col, 0).astype(F32), axis=0, keepdims=True
        ).astype(jnp.int32)
        before = jnp.where((owner_col == owner_row) & (t_row < t_col), 1.0, 0.0)
        rank_col = jnp.sum(before, axis=1, keepdims=True).astype(jnp.int32)
        named = jnp.where(iota((dp, fetch), 0) == owner_row, row_ref[...], 0).astype(F32)
        placed = jnp.where(iota((fetch, width), 1) == rank_col, 1.0, 0.0)
        asked = jnp.dot(
            named, placed, preferred_element_type=F32, precision=lax.Precision.HIGHEST
        )
        spread = jnp.where(iota((cpo, width), 1) == iota((cpo, width), 0) + cand_at, 1.0, 0.0)
        asked += jnp.dot(
            cand_ref[0].astype(F32), spread, preferred_element_type=F32,
            precision=lax.Precision.HIGHEST,
        )
        slot_col = owner_col * slots + rank_col
        slot_row = jnp.sum(
            jnp.where(
                iota((fetch, width), 1) == iota((fetch, width), 0) + slots, slot_col, 0
            ).astype(F32),
            axis=0, keepdims=True,
        )
        asked = (asked + slot_row + 0.5).astype(jnp.int32)
        for o in range(dp):
            message[o] = asked[o : o + 1, :]
        requests[pl.ds(user, 1)] = message[pl.ds(user, 1)]

    @pl.when(part == last)
    def _():
        pl.semaphore_wait(barrier, dp * mp - 1)

    @pl.when(part != last)
    def _():
        pl.semaphore_wait(barrier, dp - 1 + mp - 1)

    def ask(step, p):
        u = other_user(step)
        return pltpu.make_async_remote_copy(
            src_ref=message.at[u], dst_ref=requests.at[user],
            send_sem=ask_send.at[p, step], recv_sem=ask_recv.at[step],
            device_id=(u, p), device_id_type=MESH,
        )

    @pl.when(part == last)
    def _():
        def ask_all(step, _):
            for p in range(mp):
                ask(step, p).start()
            return 0

        lax.fori_loop(1, dp, ask_all, 0)
        for p in range(mp - 1):
            ask(0, p).start()

    def heard(step, _):
        ask(step, 0).wait_recv()
        return 0

    lax.fori_loop(1, dp, heard, 0)

    @pl.when(part != last)
    def _():
        heard(0, 0)

    loads[0].wait()
    group = min(dp, 8)

    def pick(index, _):
        these = pl.ds(index * group, group)
        asked = jnp.broadcast_to(requests[these], (group, slots, width))
        shape = (group, slots, width)
        column = jnp.sum(
            jnp.where(iota(shape, 1) == iota(shape, 2), asked, 0).astype(F32),
            axis=2, keepdims=True,
        ).astype(jnp.int32)
        items = table.shape[0]
        hot = jnp.where(column == iota((group, slots, items), 2), 1.0, 0.0)
        hot = hot.reshape(group * slots, items).astype(BF16)
        rows = jnp.dot(hot, table[...], preferred_element_type=F32).astype(BF16)
        picked[these] = rows.reshape(group, slots, table.shape[1])
        return 0

    lax.fori_loop(0, dp // group, pick, 0)
    arrived[pl.ds(user, 1)] = picked[pl.ds(user, 1)]

    def deliver(step):
        u = other_user(step)
        return pltpu.make_async_remote_copy(
            src_ref=picked.at[u], dst_ref=arrived.at[user],
            send_sem=row_send.at[step], recv_sem=row_recv.at[step],
            device_id=(u, part), device_id_type=MESH,
        )

    def deliver_start(step, _):
        deliver(step).start()
        return 0

    def deliver_wait(step, _):
        deliver(step).wait_recv()
        return 0

    lax.fori_loop(1, dp, deliver_start, 0)
    mine = jnp.broadcast_to(requests[user], (fetch, width))
    at = (fetch, width)
    slot_col = jnp.sum(
        jnp.where(iota(at, 1) == iota(at, 0) + slots, mine, 0).astype(F32),
        axis=1, keepdims=True,
    ).astype(jnp.int32)
    chosen = jnp.where(slot_col == iota((fetch, dp * slots), 1), 1.0, 0.0).astype(BF16)
    loads[1].wait()
    lax.fori_loop(1, dp, deliver_wait, 0)

    everything = arrived[...].reshape(dp * slots, arrived.shape[2])
    embedded = jnp.dot(chosen, everything, preferred_element_type=F32).astype(BF16)
    hidden = jnp.dot(embedded, w_in[...], preferred_element_type=F32).astype(BF16)

    loads[2].wait()
    loads[3].wait()
    loads[4].wait()
    sends = []
    for block, parts in enumerate((parts0, parts1, parts2, parts3)):
        gap = DILATIONS[block]
        keep = parts.shape[1]
        rows = hidden.shape[0]
        total = jnp.dot(hidden, conv_a[block, 0], preferred_element_type=F32)
        for tap in (1, 2):
            total += pltpu.roll(
                jnp.dot(hidden, conv_a[block, tap], preferred_element_type=F32),
                tap * gap, 0,
            )
        rectified = jnp.maximum(total, 0.0).astype(BF16).astype(F32)
        branch = jnp.dot(
            rectified[rows - keep :].astype(BF16), conv_b[block, 0], preferred_element_type=F32
        )
        for tap in (1, 2):
            branch += jnp.dot(
                pltpu.roll(rectified, tap * 2 * gap, 0)[rows - keep :].astype(BF16),
                conv_b[block, tap],
                preferred_element_type=F32,
            )
        parts[part] = branch.astype(BF16)
        copies = [
            pltpu.make_async_remote_copy(
                src_ref=parts.at[part], dst_ref=parts.at[part],
                send_sem=part_send.at[block, step], recv_sem=part_recv.at[block, step],
                device_id=(user, other_part(step)), device_id_type=MESH,
            )
            for step in range(1, mp)
        ]
        for copy in copies:
            copy.start()
        for copy in copies:
            copy.wait_recv()
        sends += copies
        added = parts[0].astype(F32)
        for p in range(1, mp):
            added += parts[p].astype(F32)
        summed = hidden[rows - keep :].astype(F32) + added
        mean = jnp.mean(summed, axis=1, keepdims=True)
        square = jnp.mean(summed * summed, axis=1, keepdims=True)
        normed = (summed - mean) * lax.rsqrt(square - mean * mean + 1e-5)
        hidden = (normed * gains_ref[block : block + 1, :]).astype(BF16)

    vectors = jnp.dot(hidden, w_out[...], preferred_element_type=F32)
    vector = vectors.astype(BF16).astype(F32)[hidden.shape[0] - 1 :, :]
    wanted = arrived[...].astype(F32)[:, cand_at : cand_at + cpo, :]
    raw = 0.25 * jnp.sum(wanted * vector[None], axis=2, keepdims=True)
    cube = (dp, cpo, cpo)
    raw = jnp.sum(jnp.where(iota(cube, 1) == iota(cube, 2), raw, 0.0), axis=1)
    count = jnp.sum(
        jnp.where(iota((dp, dp), 0) == iota((dp, dp), 1), count_ref[...], 0).astype(F32),
        axis=1, keepdims=True,
    ).astype(jnp.int32)
    slot = iota((dp, cpo), 1)
    live = slot < count
    scores_ref[0] = jnp.where(live, raw, 0.0)
    exp_total = jnp.sum(
        jnp.sum(jnp.where(live, jnp.exp(raw), 0.0), axis=1, keepdims=True), axis=0, keepdims=True
    )
    is_positive = (iota((dp, cpo), 0) == pos_ref[...]) & (slot == 0)
    positive = jnp.sum(
        jnp.sum(jnp.where(is_positive, raw, 0.0), axis=1, keepdims=True), axis=0, keepdims=True
    )
    loss_ref[...] = jnp.log(exp_total) - positive

    for copy in sends:
        copy.wait_send()

    def delivered(step, _):
        deliver(step).wait_send()
        return 0

    lax.fori_loop(1, dp, delivered, 0)

    @pl.when(part == last)
    def _():
        def asked_all(step, _):
            for p in range(mp):
                ask(step, p).wait_send()
            return 0

        lax.fori_loop(1, dp, asked_all, 0)
        for p in range(mp - 1):
            ask(0, p).wait_send()


def per_device(
    item_table, history_owner, history_row, w_in, conv_a, conv_b, gains, w_out,
    cand_row, cand_count, pos_owner,
):
    dp = lax.axis_size("dp")
    mp = lax.axis_size("mp")
    fetch = history_row.shape[0]
    embed = item_table.shape[1]
    channels = w_in.shape[1]
    cpo = cand_row.shape[2]
    capacity = max(4, 2 * fetch // dp)
    cand_at = round_up(capacity, 8)
    slots = round_up(cand_at + cpo, 16)
    width = round_up(slots + fetch, 128)
    assert cand_row.shape[0] == 1 and fetch > 6 * sum(DILATIONS)
    vmem = pl.BlockSpec(memory_space=pltpu.VMEM)
    hbm = pl.BlockSpec(memory_space=pl.ANY)
    scores, loss = pl.pallas_call(
        functools.partial(kernel, dp, mp, capacity, cand_at, slots),
        out_shape=(
            jax.ShapeDtypeStruct((1, dp, cpo), F32),
            jax.ShapeDtypeStruct((1, 1), F32),
        ),
        in_specs=[vmem] * 6 + [hbm] * 5,
        out_specs=(vmem, vmem),
        scratch_shapes=[
            pltpu.VMEM(item_table.shape, BF16),
            pltpu.VMEM(w_in.shape, BF16),
            pltpu.VMEM(conv_a.shape, BF16),
            pltpu.VMEM(conv_b.shape, BF16),
            pltpu.VMEM(w_out.shape, BF16),
            pltpu.VMEM((dp, 1, width), jnp.int32),
            pltpu.VMEM((dp, 1, width), jnp.int32),
            pltpu.VMEM((dp, slots, embed), BF16),
            pltpu.VMEM((dp, slots, embed), BF16),
        ]
        + [pltpu.VMEM((mp, rows_after(b), channels), BF16) for b in range(len(DILATIONS))]
        + [
            pltpu.SemaphoreType.DMA((5,)),
            pltpu.SemaphoreType.DMA((mp, dp)),
            pltpu.SemaphoreType.DMA((dp,)),
            pltpu.SemaphoreType.DMA((dp,)),
            pltpu.SemaphoreType.DMA((dp,)),
            pltpu.SemaphoreType.DMA((len(DILATIONS), mp)),
            pltpu.SemaphoreType.DMA((len(DILATIONS), mp)),
        ],
        compiler_params=pltpu.CompilerParams(
            collective_id=0, has_side_effects=True, vmem_limit_bytes=48 << 20
        ),
    )(
        history_owner, history_row.reshape(1, fetch), cand_row, cand_count,
        pos_owner.reshape(1, 1), gains, item_table, w_in, conv_a, conv_b, w_out,
    )
    return scores, loss.reshape(1)


def solution(mesh):
    return jax.shard_map(
        per_device,
        mesh=mesh,
        in_specs=(
            P("dp", None),
            P(("dp", "mp"), None),
            P(("dp", "mp")),
            P(),
            P(None, None, None, "mp"),
            P(None, None, "mp", None),
            P(),
            P(),
            P("dp", None, None),
            P("dp", None),
            P("dp"),
        ),
        out_specs=(P("dp", None, None), P("dp")),
        check_vma=False,
    )
```

time: 207 us -> 45.8 us (0.22)
  waiting for transfers between devices: 79.3 us -> 0 us
  blocking collectives: 52 us -> 0 us
  Pallas kernels: 0 us -> 32.3 us
  starting transfers between devices: 19.7 us -> 0 us
  local copies, waits for them, and re-layouts: 28.2 us -> 9.97 us
  between operations: 17.3 us -> 3.05 us
  other arithmetic: 4.98 us -> 0 us
  matrix products: 4.08 us -> 0 us
    unnamed x8 -> x0, waiting for transfers between devices: 64 us -> none
    pallas_call x0 -> x1, Pallas kernels: none -> 32.3 us  [per_device(): pl.pallas_call(functools.partial(kernel, dp, mp, capacity, cand_at, slots...]
    all_gather x5 -> x0, blocking collectives: 29 us -> none  [the longest x4 23.5 us: per_device(): hidden = lax.all_gather(normed, 'mp', axis=1, tiled=True)]
    psum x4 -> x0, blocking collectives: 23 us -> none  [per_device(): lax.psum((jnp.sum(summed, axis=1), jnp.sum(summed * summed, axis=1)), 'mp')]
    all_to_all x4 -> x0, starting transfers between devices: 19.6 us -> none  [the longest x1 7.28 us: lookup(): lax.all_to_all(requests, 'dp', split_axis=1, concat_axis=1, tiled=True)]
    all_to_all x4 -> x0, waiting for transfers between devices: 15.3 us -> none  [the longest x1 5.73 us: lookup(): lax.all_to_all(picked, 'dp', split_axis=1, concat_axis=1, tiled=True)]
    scatter x1 -> x0, local copies, waits for them, and re-layouts: 10.2 us -> none  [lookup(): jnp.zeros((groups * capacity, dp_count), jnp.int32).at[slot_ids, flat_owner]]
    gather x5 -> x0, local copies, waits for them, and re-layouts: 4.21 us -> none  [the longest x2 1.48 us: lookup(): item_table[lax.all_to_all(requests, 'dp', split_axis=1, concat_axis=1, ti...]
  transfers between devices with their start and end apart: 8 -> 0, of which waited for: 7 -> 0; matrix products, arithmetic and copies ran while one was open for 3% -> 0% of each run, Pallas kernels for 0% -> 0%
where the time goes in v1:
time: 45.8 us; the launch traced here: 45.4 us
  Pallas kernels  32.3 us (71%)
  local copies, waits for them, and re-layouts  9.97 us (22%)
  between operations  3.05 us (7%)
    pallas_call x1, Pallas kernels, per_device(): pl.pallas_call(functools.partial(kernel, dp, mp, capacity, cand_at, slots...  32.3 us
    unnamed x20, local copies, waits for them, and re-layouts  9.97 us

profile of v1, /device:TPU:0, one launch (start us, length us, event | category | flops | bytes accessed | tf_op | source)
XLA Modules:
  0.0 45.4 jit_solution(16400079873494315823)
XLA Ops:
  1.3 0.7 %copy.13.owner_ref = s32[64,1]{1,0:T(8,128)S(1)} copy(s32[64,1]{0,1:T(1,128)} %param.12) | data formatting | bytes 512 | tf_op args[1]
  2.0 0.0 copy-start
  2.0 1.4 %copy-done = bf16[4,3,512,128]{3,2,1,0:T(8,128)(2,1)S(1)} copy-done((bf16[4,3,512,128]{3,2,1,0:T(8,128)(2,1)S(1)}, bf16[4,3,512,128]{3,2,1,0:T(8,128)(2,1)}, u32[]{:S(2)}) %copy-start) | copy-done | bytes 1572888
  3.4 0.0 copy-start.1
  3.4 1.4 %copy-done.1 = bf16[4,3,128,512]{3,2,1,0:T(8,128)(2,1)S(1)} copy-done((bf16[4,3,128,512]{3,2,1,0:T(8,128)(2,1)S(1)}, bf16[4,3,128,512]{3,2,1,0:T(8,128)(2,1)}, u32[]{:S(2)}) %copy-start.1) | copy-done | bytes 1572888
  4.8 0.0 copy-start.2
  4.8 1.2 %copy-done.2 = bf16[2048,256]{1,0:T(8,128)(2,1)S(1)} copy-done((bf16[2048,256]{1,0:T(8,128)(2,1)S(1)}, bf16[2048,256]{1,0:T(8,128)(2,1)}, u32[]{:S(2)}) %copy-start.2) | copy-done | bytes 1048600
  6.1 0.0 copy-start.3
  6.1 0.9 %copy-done.3 = bf16[256,512]{1,0:T(8,128)(2,1)S(1)} copy-done((bf16[256,512]{1,0:T(8,128)(2,1)S(1)}, bf16[256,512]{1,0:T(8,128)(2,1)}, u32[]{:S(2)}) %copy-start.3) | copy-done | bytes 262168
  7.0 0.0 copy-start.4
  7.0 0.9 %copy-done.4 = bf16[512,256]{1,0:T(8,128)(2,1)S(1)} copy-done((bf16[512,256]{1,0:T(8,128)(2,1)S(1)}, bf16[512,256]{1,0:T(8,128)(2,1)}, u32[]{:S(2)}) %copy-start.4) | copy-done | bytes 262168
  8.0 0.0 copy-start.5
  8.0 0.7 %copy-done.5 = f32[4,512]{1,0:T(4,128)S(1)} copy-done((f32[4,512]{1,0:T(4,128)S(1)}, f32[4,512]{1,0:T(4,128)}, u32[]{:S(2)}) %copy-start.5) | copy-done | bytes 8216
  8.7 0.0 copy-start.6
  8.7 0.7 %copy-done.6 = s32[1,8,8]{2,1,0:T(8,128)S(1)} copy-done((s32[1,8,8]{2,1,0:T(8,128)S(1)}, s32[1,8,8]{2,1,0:T(8,128)}, u32[]{:S(2)}) %copy-start.6) | copy-done | bytes 280
  9.3 0.0 copy-start.7
  9.4 0.7 %copy-done.7 = s32[64]{0:T(128)S(1)} copy-done((s32[64]{0:T(128)S(1)}, s32[64]{0:T(128)}, u32[]{:S(2)}) %copy-start.7) | copy-done | bytes 280
  10.0 0.0 copy-start.8
  10.0 0.7 %copy-done.8 = s32[1,8]{1,0:T(1,128)S(1)} copy-done((s32[1,8]{1,0:T(1,128)S(1)}, s32[1,8]{1,0:T(1,128)}, u32[]{:S(2)}) %copy-start.8) | copy-done | bytes 56
  10.7 32.3 %shard_map.122 = (f32[1,8,8]{2,1,0:T(8,128)S(1)}, f32[1,1]{1,0:T(1,128)}) custom-call(s32[64,1]{1,0:T(8,128)S(1)} %copy.13.owner_ref, s32[1,64]{1,0:T(1,128)S(1)} %bitcast.4, s32[1,8,8]{2,1,0:T(8,128)S(1)} %copy-done.6, s32[1,8]{1,0:T(1,128)S(1)} %copy-done.8, s32[1,1]{1,0:T(1,128)} %bitcast.3.pos_ref, f32[4,512]{1,0:T(4,128)S(1)} %copy-done.5, ...), custom_call_target="tpu_custom_call" | custom-call | tf_op jit(solution)/shard_map/pallas_call | solution.py:309
  43.0 0.6 %copy.17 = f32[1,8,8]{2,1,0:T(8,128)} copy(f32[1,8,8]{2,1,0:T(8,128)S(1)} %get-tuple-element.8) | data formatting | bytes 512
Async XLA Ops:
  2.0 1.4 %copy-start = (bf16[4,3,512,128]{3,2,1,0:T(8,128)(2,1)S(1)}, bf16[4,3,512,128]{3,2,1,0:T(8,128)(2,1)}, u32[]{:S(2)}) copy-start(bf16[4,3,512,128]{3,2,1,0:T(8,128)(2,1)} %conv_a_hbm.1) | copy-start | bytes 4718596
  3.4 1.4 %copy-start.1 = (bf16[4,3,128,512]{3,2,1,0:T(8,128)(2,1)S(1)}, bf16[4,3,128,512]{3,2,1,0:T(8,128)(2,1)}, u32[]{:S(2)}) copy-start(bf16[4,3,128,512]{3,2,1,0:T(8,128)(2,1)} %conv_b_hbm.1) | copy-start | bytes 4718596
  4.8 1.2 %copy-start.2 = (bf16[2048,256]{1,0:T(8,128)(2,1)S(1)}, bf16[2048,256]{1,0:T(8,128)(2,1)}, u32[]{:S(2)}) copy-start(bf16[2048,256]{1,0:T(8,128)(2,1)} %table_hbm.1) | copy-start | bytes 3145732
  6.1 0.9 %copy-start.3 = (bf16[256,512]{1,0:T(8,128)(2,1)S(1)}, bf16[256,512]{1,0:T(8,128)(2,1)}, u32[]{:S(2)}) copy-start(bf16[256,512]{1,0:T(8,128)(2,1)} %w_in_hbm.1) | copy-start | bytes 786436
  7.0 0.9 %copy-start.4 = (bf16[512,256]{1,0:T(8,128)(2,1)S(1)}, bf16[512,256]{1,0:T(8,128)(2,1)}, u32[]{:S(2)}) copy-start(bf16[512,256]{1,0:T(8,128)(2,1)} %w_out_hbm.1) | copy-start | bytes 786436
  8.0 0.7 %copy-start.5 = (f32[4,512]{1,0:T(4,128)S(1)}, f32[4,512]{1,0:T(4,128)}, u32[]{:S(2)}) copy-start(f32[4,512]{1,0:T(4,128)} %gains_ref.1) | copy-start | bytes 24580
  8.7 0.7 %copy-start.6 = (s32[1,8,8]{2,1,0:T(8,128)S(1)}, s32[1,8,8]{2,1,0:T(8,128)}, u32[]{:S(2)}) copy-start(s32[1,8,8]{2,1,0:T(8,128)} %cand_ref.1) | copy-start | bytes 772
  9.3 0.7 %copy-start.7 = (s32[64]{0:T(128)S(1)}, s32[64]{0:T(128)}, u32[]{:S(2)}) copy-start(s32[64]{0:T(128)} %param.13) | copy-start | bytes 772
  10.0 0.7 %copy-start.8 = (s32[1,8]{1,0:T(1,128)S(1)}, s32[1,8]{1,0:T(1,128)}, u32[]{:S(2)}) copy-start(s32[1,8]{1,0:T(1,128)} %count_ref.1) | copy-start | bytes 100

commit v2 on v1

--- a/solution.py
+++ b/solution.py
@@ -9,6 +9,7 @@
 
 MESH = pl.DeviceIdType.MESH
 DILATIONS = (1, 4, 1, 4)
+STRIDES = (1, 1, 4, 1)
 F32 = jnp.float32
 BF16 = jnp.bfloat16
 
@@ -22,21 +23,23 @@
 
 
 def rows_after(block):
-    return round_up(1 + 6 * sum(DILATIONS[block + 1 :]), 16)
+    reach = 6 * sum(DILATIONS[block + 1 :]) // STRIDES[block]
+    return round_up(1 + reach, 16)
 
 
 def kernel(
     dp, mp, capacity, cand_at, slots,
-    owner_ref, row_ref, cand_ref, count_ref, pos_ref, gains_ref,
+    owner_hbm, row_hbm, cand_hbm, count_hbm, pos_hbm, gains_hbm,
     table_hbm, w_in_hbm, conv_a_hbm, conv_b_hbm, w_out_hbm,
     scores_ref, loss_ref,
+    owner_ref, row_ref, cand_ref, count_ref, pos_ref, gains_ref,
     table, w_in, conv_a, conv_b, w_out,
     message, requests, picked, arrived, parts0, parts1, parts2, parts3,
     load_sem, ask_send, ask_recv, row_send, row_recv, part_send, part_recv,
 ):
     user = lax.axis_index("dp")
     part = lax.axis_index("mp")
-    fetch = owner_ref.shape[0]
+    fetch = owner_ref.shape[1]
     width = message.shape[2]
     cpo = cand_ref.shape[2]
     last = mp - 1
@@ -44,8 +47,10 @@
     loads = [
         pltpu.make_async_copy(source, target, load_sem.at[i])
         for i, (source, target) in enumerate(
-            [(table_hbm, table), (w_in_hbm, w_in), (conv_a_hbm, conv_a),
-             (conv_b_hbm, conv_b), (w_out_hbm, w_out)]
+            [(owner_hbm, owner_ref), (row_hbm, row_ref), (cand_hbm, cand_ref),
+             (table_hbm, table), (w_in_hbm, w_in), (conv_a_hbm, conv_a),
+             (conv_b_hbm, conv_b), (gains_hbm, gains_ref), (w_out_hbm, w_out),
+             (count_hbm, count_ref), (pos_hbm, pos_ref)]
         )
     ]
     for load in loads:
@@ -78,13 +83,16 @@
     def _():
         lax.fori_loop(1, dp, greet_askers, 0)
 
+    for load in loads[:3]:
+        load.wait()
+
     @pl.when(part == last)
     def _():
-        owner_col = owner_ref[...]
+        owner_row = owner_ref[...]
         square = (fetch, fetch)
         t_col, t_row = iota(square, 0), iota(square, 1)
-        owner_row = jnp.sum(
-            jnp.where(t_col == t_row, owner_col, 0).astype(F32), axis=0, keepdims=True
+        owner_col = jnp.sum(
+            jnp.where(t_col == t_row, owner_row, 0).astype(F32), axis=1, keepdims=True
         ).astype(jnp.int32)
         before = jnp.where((owner_col == owner_row) & (t_row < t_col), 1.0, 0.0)
         rank_col = jnp.sum(before, axis=1, keepdims=True).astype(jnp.int32)
@@ -147,7 +155,7 @@
     def _():
         heard(0, 0)
 
-    loads[0].wait()
+    loads[3].wait()
     group = min(dp, 8)
 
     def pick(index, _):
@@ -192,21 +200,21 @@
         axis=1, keepdims=True,
     ).astype(jnp.int32)
     chosen = jnp.where(slot_col == iota((fetch, dp * slots), 1), 1.0, 0.0).astype(BF16)
-    loads[1].wait()
+    loads[4].wait()
     lax.fori_loop(1, dp, deliver_wait, 0)
 
     everything = arrived[...].reshape(dp * slots, arrived.shape[2])
     embedded = jnp.dot(chosen, everything, preferred_element_type=F32).astype(BF16)
     hidden = jnp.dot(embedded, w_in[...], preferred_element_type=F32).astype(BF16)
 
-    loads[2].wait()
-    loads[3].wait()
-    loads[4].wait()
+    for load in loads[5:]:
+        load.wait()
     sends = []
     for block, parts in enumerate((parts0, parts1, parts2, parts3)):
-        gap = DILATIONS[block]
         keep = parts.shape[1]
         rows = hidden.shape[0]
+        stride = STRIDES[block]
+        gap = DILATIONS[block] // (STRIDES[block - 1] if block else 1)
         total = jnp.dot(hidden, conv_a[block, 0], preferred_element_type=F32)
         for tap in (1, 2):
             total += pltpu.roll(
@@ -214,14 +222,20 @@
                 tap * gap, 0,
             )
         rectified = jnp.maximum(total, 0.0).astype(BF16).astype(F32)
-        branch = jnp.dot(
-            rectified[rows - keep :].astype(BF16), conv_b[block, 0], preferred_element_type=F32
-        )
-        for tap in (1, 2):
+        branch = 0.0
+        base = hidden[rows - keep :]
+        if stride > 1:
+            at = iota((keep, rows), 0) * stride + rows - 1 - (keep - 1) * stride
+            strided = jnp.where(at == iota((keep, rows), 1), 1.0, 0.0).astype(BF16)
+            base = jnp.dot(strided, hidden, preferred_element_type=F32)
+        for tap in range(3):
+            shifted = pltpu.roll(rectified, tap * 2 * gap, 0) if tap else rectified
+            if stride > 1:
+                shifted = jnp.dot(strided, shifted.astype(BF16), preferred_element_type=F32)
+            else:
+                shifted = shifted[rows - keep :]
             branch += jnp.dot(
-                pltpu.roll(rectified, tap * 2 * gap, 0)[rows - keep :].astype(BF16),
-                conv_b[block, tap],
-                preferred_element_type=F32,
+                shifted.astype(BF16), conv_b[block, tap], preferred_element_type=F32
             )
         parts[part] = branch.astype(BF16)
         copies = [
@@ -240,7 +254,7 @@
         added = parts[0].astype(F32)
         for p in range(1, mp):
             added += parts[p].astype(F32)
-        summed = hidden[rows - keep :].astype(F32) + added
+        summed = base.astype(F32) + added
         mean = jnp.mean(summed, axis=1, keepdims=True)
         square = jnp.mean(summed * summed, axis=1, keepdims=True)
         normed = (summed - mean) * lax.rsqrt(square - mean * mean + 1e-5)
@@ -312,9 +326,15 @@
             jax.ShapeDtypeStruct((1, dp, cpo), F32),
             jax.ShapeDtypeStruct((1, 1), F32),
         ),
-        in_specs=[vmem] * 6 + [hbm] * 5,
+        in_specs=[hbm] * 11,
         out_specs=(vmem, vmem),
         scratch_shapes=[
+            pltpu.VMEM((1, fetch), jnp.int32),
+            pltpu.VMEM((1, fetch), jnp.int32),
+            pltpu.VMEM(cand_row.shape, jnp.int32),
+            pltpu.VMEM(cand_count.shape, jnp.int32),
+            pltpu.VMEM((1, 1), jnp.int32),
+            pltpu.VMEM(gains.shape, F32),
             pltpu.VMEM(item_table.shape, BF16),
             pltpu.VMEM(w_in.shape, BF16),
             pltpu.VMEM(conv_a.shape, BF16),
@@ -327,7 +347,7 @@
         ]
         + [pltpu.VMEM((mp, rows_after(b), channels), BF16) for b in range(len(DILATIONS))]
         + [
-            pltpu.SemaphoreType.DMA((5,)),
+            pltpu.SemaphoreType.DMA((11,)),
             pltpu.SemaphoreType.DMA((mp, dp)),
             pltpu.SemaphoreType.DMA((dp,)),
             pltpu.SemaphoreType.DMA((dp,)),
@@ -336,10 +356,10 @@
             pltpu.SemaphoreType.DMA((len(DILATIONS), mp)),
         ],
         compiler_params=pltpu.CompilerParams(
-            collective_id=0, has_side_effects=True, vmem_limit_bytes=48 << 20
+            collective_id=0, has_side_effects=True, vmem_limit_bytes=60 << 20
         ),
     )(
-        history_owner, history_row.reshape(1, fetch), cand_row, cand_count,
+        history_owner.reshape(1, fetch), history_row.reshape(1, fetch), cand_row, cand_count,
         pos_owner.reshape(1, 1), gains, item_table, w_in, conv_a, conv_b, w_out,
     )
     return scores, loss.reshape(1)

time: 45.8 us -> 36.5 us (0.80)
  local copies, waits for them, and re-layouts: 9.97 us -> 1.26 us
    unnamed x20 -> x1, local copies, waits for them, and re-layouts: 9.97 us -> 1.26 us
where the time goes in v2:
time: 36.5 us; the launch traced here: 36.2 us
  Pallas kernels  31.9 us (87%)
  between operations  3.05 us (8%)
  local copies, waits for them, and re-layouts  1.26 us (3%)
    pallas_call x1, Pallas kernels, per_device(): pl.pallas_call(functools.partial(kernel, dp, mp, capacity, cand_at, slots...  31.9 us
    unnamed x1, local copies, waits for them, and re-layouts  1.26 us

profile of v2, /device:TPU:0, one launch (start us, length us, event | category | flops | bytes accessed | tf_op | source)
XLA Modules:
  0.0 36.2 jit_solution(6439737906818176533)
XLA Ops:
  1.3 31.9 %shard_map.122 = (f32[1,8,8]{2,1,0:T(8,128)}, f32[1,1]{1,0:T(1,128)}) custom-call(s32[1,64]{1,0:T(1,128)} %bitcast.5, s32[1,64]{1,0:T(1,128)} %bitcast.6, s32[1,8,8]{2,1,0:T(8,128)} %cand_hbm.1, s32[1,8]{1,0:T(1,128)} %count_hbm.1, s32[1,1]{1,0:T(1,128)} %bitcast.4.pos_hbm, f32[4,512]{1,0:T(4,128)} %gains_hbm.1, bf16[2048,256]{1,0:T(8,128)(2,1)} %table_hbm.1, ...), custom_call_target="tpu_custom_call" | custom-call | tf_op jit(solution)/shard_map/pallas_call | solution.py:323
  33.2 1.3 %copy.16 = f32[1,8,8]{2,1,0:T(8,128)} copy(f32[1,8,8]{2,1,0:T(8,128)} %get-tuple-element.8) | data formatting | bytes 512

commit v3 on v2

--- a/solution.py
+++ b/solution.py
@@ -28,13 +28,13 @@
 
 
 def kernel(
-    dp, mp, capacity, cand_at, slots,
+    dp, mp, cand_at, slots,
     owner_hbm, row_hbm, cand_hbm, count_hbm, pos_hbm, gains_hbm,
     table_hbm, w_in_hbm, conv_a_hbm, conv_b_hbm, w_out_hbm,
     scores_ref, loss_ref,
     owner_ref, row_ref, cand_ref, count_ref, pos_ref, gains_ref,
     table, w_in, conv_a, conv_b, w_out,
-    message, requests, picked, arrived, parts0, parts1, parts2, parts3,
+    message, requests, picked, arrived, cand_picked, cand_arrived, parts0, parts1, parts2, parts3,
     load_sem, ask_send, ask_recv, row_send, row_recv, part_send, part_recv,
 ):
     user = lax.axis_index("dp")
@@ -106,7 +106,7 @@
             cand_ref[0].astype(F32), spread, preferred_element_type=F32,
             precision=lax.Precision.HIGHEST,
         )
-        slot_col = owner_col * slots + rank_col
+        slot_col = owner_col * cand_at + rank_col
         slot_row = jnp.sum(
             jnp.where(
                 iota((fetch, width), 1) == iota((fetch, width), 0) + slots, slot_col, 0
@@ -158,52 +158,62 @@
     loads[3].wait()
     group = min(dp, 8)
 
-    def pick(index, _):
-        these = pl.ds(index * group, group)
-        asked = jnp.broadcast_to(requests[these], (group, slots, width))
-        shape = (group, slots, width)
-        column = jnp.sum(
-            jnp.where(iota(shape, 1) == iota(shape, 2), asked, 0).astype(F32),
-            axis=2, keepdims=True,
-        ).astype(jnp.int32)
-        items = table.shape[0]
-        hot = jnp.where(column == iota((group, slots, items), 2), 1.0, 0.0)
-        hot = hot.reshape(group * slots, items).astype(BF16)
-        rows = jnp.dot(hot, table[...], preferred_element_type=F32).astype(BF16)
-        picked[these] = rows.reshape(group, slots, table.shape[1])
-        return 0
-
-    lax.fori_loop(0, dp // group, pick, 0)
-    arrived[pl.ds(user, 1)] = picked[pl.ds(user, 1)]
-
-    def deliver(step):
+    def pick(first, target):
+        count = target.shape[1]
+
+        def step(index, _):
+            these = pl.ds(index * group, group)
+            shape = (group, count, width)
+            asked = jnp.broadcast_to(requests[these], shape)
+            column = jnp.sum(
+                jnp.where(iota(shape, 1) + first == iota(shape, 2), asked, 0).astype(F32),
+                axis=2, keepdims=True,
+            ).astype(jnp.int32)
+            items = table.shape[0]
+            hot = jnp.where(column == iota((group, count, items), 2), 1.0, 0.0)
+            hot = hot.reshape(group * count, items).astype(BF16)
+            rows = jnp.dot(hot, table[...], preferred_element_type=F32).astype(BF16)
+            target[these] = rows.reshape(group, count, table.shape[1])
+            return 0
+
+        if dp == group:
+            step(0, 0)
+        else:
+            lax.fori_loop(0, dp // group, step, 0)
+
+    def deliver(kind, step):
+        source, target = ((picked, arrived), (cand_picked, cand_arrived))[kind]
         u = other_user(step)
         return pltpu.make_async_remote_copy(
-            src_ref=picked.at[u], dst_ref=arrived.at[user],
-            send_sem=row_send.at[step], recv_sem=row_recv.at[step],
+            src_ref=source.at[u], dst_ref=target.at[user],
+            send_sem=row_send.at[kind, step], recv_sem=row_recv.at[kind, step],
             device_id=(u, part), device_id_type=MESH,
         )
 
-    def deliver_start(step, _):
-        deliver(step).start()
-        return 0
-
-    def deliver_wait(step, _):
-        deliver(step).wait_recv()
-        return 0
-
-    lax.fori_loop(1, dp, deliver_start, 0)
+    def for_others(act):
+        def body(step, _):
+            act(step)
+            return 0
+
+        lax.fori_loop(1, dp, body, 0)
+
+    pick(0, picked)
+    for_others(lambda step: deliver(0, step).start())
+    arrived[pl.ds(user, 1)] = picked[pl.ds(user, 1)]
+    pick(cand_at, cand_picked)
+    for_others(lambda step: deliver(1, step).start())
+    cand_arrived[pl.ds(user, 1)] = cand_picked[pl.ds(user, 1)]
     mine = jnp.broadcast_to(requests[user], (fetch, width))
     at = (fetch, width)
     slot_col = jnp.sum(
         jnp.where(iota(at, 1) == iota(at, 0) + slots, mine, 0).astype(F32),
         axis=1, keepdims=True,
     ).astype(jnp.int32)
-    chosen = jnp.where(slot_col == iota((fetch, dp * slots), 1), 1.0, 0.0).astype(BF16)
+    chosen = jnp.where(slot_col == iota((fetch, dp * cand_at), 1), 1.0, 0.0).astype(BF16)
     loads[4].wait()
-    lax.fori_loop(1, dp, deliver_wait, 0)
-
-    everything = arrived[...].reshape(dp * slots, arrived.shape[2])
+    for_others(lambda step: deliver(0, step).wait_recv())
+
+    everything = arrived[...].reshape(dp * cand_at, arrived.shape[2])
     embedded = jnp.dot(chosen, everything, preferred_element_type=F32).astype(BF16)
     hidden = jnp.dot(embedded, w_in[...], preferred_element_type=F32).astype(BF16)
 
@@ -262,7 +272,8 @@
 
     vectors = jnp.dot(hidden, w_out[...], preferred_element_type=F32)
     vector = vectors.astype(BF16).astype(F32)[hidden.shape[0] - 1 :, :]
-    wanted = arrived[...].astype(F32)[:, cand_at : cand_at + cpo, :]
+    for_others(lambda step: deliver(1, step).wait_recv())
+    wanted = cand_arrived[...].astype(F32)[:, :cpo, :]
     raw = 0.25 * jnp.sum(wanted * vector[None], axis=2, keepdims=True)
     cube = (dp, cpo, cpo)
     raw = jnp.sum(jnp.where(iota(cube, 1) == iota(cube, 2), raw, 0.0), axis=1)
@@ -276,7 +287,7 @@
     exp_total = jnp.sum(
         jnp.sum(jnp.where(live, jnp.exp(raw), 0.0), axis=1, keepdims=True), axis=0, keepdims=True
     )
-    is_positive = (iota((dp, cpo), 0) == pos_ref[...]) & (slot == 0)
+    is_positive = (iota((dp, cpo), 0) == pos_ref[0]) & (slot == 0)
     positive = jnp.sum(
         jnp.sum(jnp.where(is_positive, raw, 0.0), axis=1, keepdims=True), axis=0, keepdims=True
     )
@@ -285,11 +296,8 @@
     for copy in sends:
         copy.wait_send()
 
-    def delivered(step, _):
-        deliver(step).wait_send()
-        return 0
-
-    lax.fori_loop(1, dp, delivered, 0)
+    for_others(lambda step: deliver(0, step).wait_send())
+    for_others(lambda step: deliver(1, step).wait_send())
 
     @pl.when(part == last)
     def _():
@@ -314,14 +322,15 @@
     channels = w_in.shape[1]
     cpo = cand_row.shape[2]
     capacity = max(4, 2 * fetch // dp)
-    cand_at = round_up(capacity, 8)
-    slots = round_up(cand_at + cpo, 16)
+    cand_at = round_up(capacity, 16)
+    cand_rows = round_up(cpo, 16)
+    slots = cand_at + cand_rows
     width = round_up(slots + fetch, 128)
     assert cand_row.shape[0] == 1 and fetch > 6 * sum(DILATIONS)
     vmem = pl.BlockSpec(memory_space=pltpu.VMEM)
     hbm = pl.BlockSpec(memory_space=pl.ANY)
     scores, loss = pl.pallas_call(
-        functools.partial(kernel, dp, mp, capacity, cand_at, slots),
+        functools.partial(kernel, dp, mp, cand_at, slots),
         out_shape=(
             jax.ShapeDtypeStruct((1, dp, cpo), F32),
             jax.ShapeDtypeStruct((1, 1), F32),
@@ -333,7 +342,7 @@
             pltpu.VMEM((1, fetch), jnp.int32),
             pltpu.VMEM(cand_row.shape, jnp.int32),
             pltpu.VMEM(cand_count.shape, jnp.int32),
-            pltpu.VMEM((1, 1), jnp.int32),
+            pltpu.SMEM((1,), jnp.int32),
             pltpu.VMEM(gains.shape, F32),
             pltpu.VMEM(item_table.shape, BF16),
             pltpu.VMEM(w_in.shape, BF16),
@@ -342,16 +351,18 @@
             pltpu.VMEM(w_out.shape, BF16),
             pltpu.VMEM((dp, 1, width), jnp.int32),
             pltpu.VMEM((dp, 1, width), jnp.int32),
-            pltpu.VMEM((dp, slots, embed), BF16),
-            pltpu.VMEM((dp, slots, embed), BF16),
+            pltpu.VMEM((dp, cand_at, embed), BF16),
+            pltpu.VMEM((dp, cand_at, embed), BF16),
+            pltpu.VMEM((dp, cand_rows, embed), BF16),
+            pltpu.VMEM((dp, cand_rows, embed), BF16),
         ]
         + [pltpu.VMEM((mp, rows_after(b), channels), BF16) for b in range(len(DILATIONS))]
         + [
             pltpu.SemaphoreType.DMA((11,)),
             pltpu.SemaphoreType.DMA((mp, dp)),
             pltpu.SemaphoreType.DMA((dp,)),
-            pltpu.SemaphoreType.DMA((dp,)),
-            pltpu.SemaphoreType.DMA((dp,)),
+            pltpu.SemaphoreType.DMA((2, dp)),
+            pltpu.SemaphoreType.DMA((2, dp)),
             pltpu.SemaphoreType.DMA((len(DILATIONS), mp)),
             pltpu.SemaphoreType.DMA((len(DILATIONS), mp)),
         ],
@@ -360,7 +371,7 @@
         ),
     )(
         history_owner.reshape(1, fetch), history_row.reshape(1, fetch), cand_row, cand_count,
-        pos_owner.reshape(1, 1), gains, item_table, w_in, conv_a, conv_b, w_out,
+        pos_owner, gains, item_table, w_in, conv_a, conv_b, w_out,
     )
     return scores, loss.reshape(1)
 

time: 36.5 us -> 36.1 us (0.989)
  no operation moved by 1% of the time
where the time goes in v3:
time: 36.1 us; the launch traced here: 35.9 us
  Pallas kernels  31.6 us (88%)
  between operations  3.05 us (8%)
  local copies, waits for them, and re-layouts  1.26 us (3%)
    pallas_call x1, Pallas kernels, per_device(): pl.pallas_call(functools.partial(kernel, dp, mp, cand_at, slots), out_sha...  31.6 us
    unnamed x1, local copies, waits for them, and re-layouts  1.26 us

profile of v3, /device:TPU:0, one launch (start us, length us, event | category | flops | bytes accessed | tf_op | source)
XLA Modules:
  0.0 35.9 jit_solution(6105817450825415180)
XLA Ops:
  1.3 31.6 %shard_map.122 = (f32[1,8,8]{2,1,0:T(8,128)}, f32[1,1]{1,0:T(1,128)}) custom-call(s32[1,64]{1,0:T(1,128)} %bitcast.3, s32[1,64]{1,0:T(1,128)} %bitcast.4, s32[1,8,8]{2,1,0:T(8,128)} %cand_hbm.1, s32[1,8]{1,0:T(1,128)} %count_hbm.1, s32[1]{0:T(128)S(6)} %copy.15.pos_hbm, f32[4,512]{1,0:T(4,128)} %gains_hbm.1, bf16[2048,256]{1,0:T(8,128)(2,1)} %table_hbm.1, ...), custom_call_target="tpu_custom_call" | custom-call | tf_op jit(solution)/shard_map/pallas_call | solution.py:332
  32.9 1.3 %copy.16 = f32[1,8,8]{2,1,0:T(8,128)} copy(f32[1,8,8]{2,1,0:T(8,128)} %get-tuple-element.8) | data formatting | bytes 512

commit v4 on v3

--- a/solution.py
+++ b/solution.py
@@ -22,6 +22,14 @@
     return lax.broadcasted_iota(jnp.int32, shape, axis)
 
 
+def others(dp, body):
+    if dp <= 8:
+        for step in range(1, dp):
+            body(step, 0)
+    else:
+        lax.fori_loop(1, dp, body, 0)
+
+
 def rows_after(block):
     reach = 6 * sum(DILATIONS[block + 1 :]) // STRIDES[block]
     return round_up(1 + reach, 16)
@@ -31,7 +39,7 @@
     dp, mp, cand_at, slots,
     owner_hbm, row_hbm, cand_hbm, count_hbm, pos_hbm, gains_hbm,
     table_hbm, w_in_hbm, conv_a_hbm, conv_b_hbm, w_out_hbm,
-    scores_ref, loss_ref,
+    result_ref,
     owner_ref, row_ref, cand_ref, count_ref, pos_ref, gains_ref,
     table, w_in, conv_a, conv_b, w_out,
     message, requests, picked, arrived, cand_picked, cand_arrived, parts0, parts1, parts2, parts3,
@@ -75,13 +83,13 @@
         greet(other_user(step), last)
         return 0
 
-    lax.fori_loop(1, dp, greet_same_part, 0)
+    others(dp, greet_same_part)
     for step in range(1, mp):
         greet(user, other_part(step))
 
     @pl.when(part != last)
     def _():
-        lax.fori_loop(1, dp, greet_askers, 0)
+        others(dp, greet_askers)
 
     for load in loads[:3]:
         load.wait()
@@ -141,7 +149,7 @@
                 ask(step, p).start()
             return 0
 
-        lax.fori_loop(1, dp, ask_all, 0)
+        others(dp, ask_all)
         for p in range(mp - 1):
             ask(0, p).start()
 
@@ -149,7 +157,7 @@
         ask(step, 0).wait_recv()
         return 0
 
-    lax.fori_loop(1, dp, heard, 0)
+    others(dp, heard)
 
     @pl.when(part != last)
     def _():
@@ -195,7 +203,7 @@
             act(step)
             return 0
 
-        lax.fori_loop(1, dp, body, 0)
+        others(dp, body)
 
     pick(0, picked)
     for_others(lambda step: deliver(0, step).start())
@@ -283,7 +291,7 @@
     ).astype(jnp.int32)
     slot = iota((dp, cpo), 1)
     live = slot < count
-    scores_ref[0] = jnp.where(live, raw, 0.0)
+    scores = jnp.where(live, raw, 0.0)
     exp_total = jnp.sum(
         jnp.sum(jnp.where(live, jnp.exp(raw), 0.0), axis=1, keepdims=True), axis=0, keepdims=True
     )
@@ -291,7 +299,9 @@
     positive = jnp.sum(
         jnp.sum(jnp.where(is_positive, raw, 0.0), axis=1, keepdims=True), axis=0, keepdims=True
     )
-    loss_ref[...] = jnp.log(exp_total) - positive
+    loss = jnp.broadcast_to(jnp.log(exp_total) - positive, (dp, cpo))
+    result_ref[0, :, :cpo] = scores
+    result_ref[0, :, cpo:] = loss
 
     for copy in sends:
         copy.wait_send()
@@ -306,7 +316,7 @@
                 ask(step, p).wait_send()
             return 0
 
-        lax.fori_loop(1, dp, asked_all, 0)
+        others(dp, asked_all)
         for p in range(mp - 1):
             ask(0, p).wait_send()
 
@@ -329,14 +339,11 @@
     assert cand_row.shape[0] == 1 and fetch > 6 * sum(DILATIONS)
     vmem = pl.BlockSpec(memory_space=pltpu.VMEM)
     hbm = pl.BlockSpec(memory_space=pl.ANY)
-    scores, loss = pl.pallas_call(
+    result = pl.pallas_call(
         functools.partial(kernel, dp, mp, cand_at, slots),
-        out_shape=(
-            jax.ShapeDtypeStruct((1, dp, cpo), F32),
-            jax.ShapeDtypeStruct((1, 1), F32),
-        ),
+        out_shape=jax.ShapeDtypeStruct((1, dp, 2 * cpo), F32),
         in_specs=[hbm] * 11,
-        out_specs=(vmem, vmem),
+        out_specs=vmem,
         scratch_shapes=[
             pltpu.VMEM((1, fetch), jnp.int32),
             pltpu.VMEM((1, fetch), jnp.int32),
@@ -373,7 +380,7 @@
         history_owner.reshape(1, fetch), history_row.reshape(1, fetch), cand_row, cand_count,
         pos_owner, gains, item_table, w_in, conv_a, conv_b, w_out,
     )
-    return scores, loss.reshape(1)
+    return result[:, :, :cpo], result[:, 0, cpo]
 
 
 def solution(mesh):

time: 36.1 us -> 35.5 us (0.983)
  between operations: 3.05 us -> 1.29 us
  local copies, waits for them, and re-layouts: 1.26 us -> 2.54 us
    slice x0 -> x1, local copies, waits for them, and re-layouts: none -> 1.26 us  [per_device(): return (result[:, :, :cpo], result[:, 0, cpo])]
where the time goes in v4:
time: 35.5 us; the launch traced here: 35.3 us
  Pallas kernels  31.5 us (89%)
  local copies, waits for them, and re-layouts  2.54 us (7%)
  between operations  1.29 us (4%)
    pallas_call x1, Pallas kernels, per_device(): pl.pallas_call(functools.partial(kernel, dp, mp, cand_at, slots), out_sha...  31.5 us
    unnamed x1, local copies, waits for them, and re-layouts  1.27 us
    slice x1, local copies, waits for them, and re-layouts, per_device(): return (result[:, :, :cpo], result[:, 0, cpo])  1.26 us

profile of v4, /device:TPU:0, one launch (start us, length us, event | category | flops | bytes accessed | tf_op | source)
XLA Modules:
  0.0 35.3 jit_solution(15762724949687252824)
XLA Ops:
  1.3 31.5 %shard_map.122 = f32[1,8,16]{2,1,0:T(8,128)} custom-call(s32[1,64]{1,0:T(1,128)} %bitcast.5, s32[1,64]{1,0:T(1,128)} %bitcast.6, s32[1,8,8]{2,1,0:T(8,128)} %cand_hbm.1, s32[1,8]{1,0:T(1,128)} %count_hbm.1, s32[1]{0:T(128)S(6)} %copy.14.pos_hbm, f32[4,512]{1,0:T(4,128)} %gains_hbm.1, bf16[2048,256]{1,0:T(8,128)(2,1)} %table_hbm.1, ...), custom_call_target="tpu_custom_call" | custom-call | tf_op jit(solution)/shard_map/pallas_call | solution.py:342
  32.8 1.3 %slice.7 = f32[1,1,1]{2,1,0:T(1,128)} slice(f32[1,8,16]{2,1,0:T(8,128)} %shard_map.122), slice={[0:1], [0:1], [8:9]} | slice | bytes 8 | tf_op jit(solution)/shard_map/slice | solution.py:383
  34.0 1.3 %copy.15 = f32[1,8,8]{2,1,0:T(8,128)} copy(f32[1,8,8]{2,1,0:T(8,128)} %bitcast.4) | data formatting | bytes 512

commit v5 on v4

--- a/solution.py
+++ b/solution.py
@@ -24,7 +24,7 @@
 
 def others(dp, body):
     if dp <= 8:
-        for step in range(1, dp):
+        for step in sorted(range(1, dp), key=lambda step: -min(step, dp - step)):
             body(step, 0)
     else:
         lax.fori_loop(1, dp, body, 0)
@@ -262,7 +262,7 @@
                 send_sem=part_send.at[block, step], recv_sem=part_recv.at[block, step],
                 device_id=(user, other_part(step)), device_id_type=MESH,
             )
-            for step in range(1, mp)
+            for step in sorted(range(1, mp), key=lambda step: -min(step, mp - step))
         ]
         for copy in copies:
             copy.start()

time: 35.5 us -> 36.5 us (1.028)
  Pallas kernels: 31.5 us -> 32.4 us
    pallas_call x1, Pallas kernels: 31.5 us -> 32.4 us  [per_device(): pl.pallas_call(functools.partial(kernel, dp, mp, cand_at, slots), out_sha...]
where the time goes in v5:
time: 36.5 us; the launch traced here: 36.2 us
  Pallas kernels  32.4 us (89%)
  local copies, waits for them, and re-layouts  2.54 us (7%)
  between operations  1.29 us (4%)
    pallas_call x1, Pallas kernels, per_device(): pl.pallas_call(functools.partial(kernel, dp, mp, cand_at, slots), out_sha...  32.4 us
    unnamed x1, local copies, waits for them, and re-layouts  1.27 us
    slice x1, local copies, waits for them, and re-layouts, per_device(): return (result[:, :, :cpo], result[:, 0, cpo])  1.26 us

profile of v5, /device:TPU:0, one launch (start us, length us, event | category | flops | bytes accessed | tf_op | source)
XLA Modules:
  0.0 36.2 jit_solution(16830900895658624542)
XLA Ops:
  1.3 32.4 %shard_map.122 = f32[1,8,16]{2,1,0:T(8,128)} custom-call(s32[1,64]{1,0:T(1,128)} %bitcast.5, s32[1,64]{1,0:T(1,128)} %bitcast.6, s32[1,8,8]{2,1,0:T(8,128)} %cand_hbm.1, s32[1,8]{1,0:T(1,128)} %count_hbm.1, s32[1]{0:T(128)S(6)} %copy.14.pos_hbm, f32[4,512]{1,0:T(4,128)} %gains_hbm.1, bf16[2048,256]{1,0:T(8,128)(2,1)} %table_hbm.1, ...), custom_call_target="tpu_custom_call" | custom-call | tf_op jit(solution)/shard_map/pallas_call | solution.py:342
  33.7 1.3 %slice.7 = f32[1,1,1]{2,1,0:T(1,128)} slice(f32[1,8,16]{2,1,0:T(8,128)} %shard_map.122), slice={[0:1], [0:1], [8:9]} | slice | bytes 8 | tf_op jit(solution)/shard_map/slice | solution.py:383
  35.0 1.3 %copy.15 = f32[1,8,8]{2,1,0:T(8,128)} copy(f32[1,8,8]{2,1,0:T(8,128)} %bitcast.4) | data formatting | bytes 512
